TPU v7x, 1024 devices: a whole 8x8x8 slice. The times are simulated.
1024 devices in a mesh: grid: 32 (over x, z_lo), interp: 32 (over y, z_hi, core).
Axes of the slice: x: 8, y: 8, z: 8 (z_hi: 2, z_lo: 4; z = z_hi * 4 + z_lo), core: 2. Of those that a mesh axis runs over, the one named last changes fastest.
Arguments:
- valence: bfloat16 [262144, 512], P(('grid', 'interp')), may hold values from -1.296875 to 1.296875
- conduction: bfloat16 [262144, 512], P(('grid', 'interp')), may hold values from -1.296875 to 1.296875
- points: int32 [16384], P('grid'), may hold values from 0 to 262143, as said below
- inverse_metric: bfloat16 [16384, 16384], P('grid', 'interp'), as said below
Outputs:
- fitting: bfloat16 [1024, 16384], P('grid', 'interp')
Inputs may be any that keep to these rules, and one draw needn't show every extreme that they name: Entries k * 512 to (k + 1) * 512 - 1 of points are distinct grid points of slab k, that is of k * 8192 to (k + 1) * 8192 - 1, and include that slab's first and last point. `inverse_metric`: A diagonal between 0.5 and 2 with small dense entries off it, of standard deviation about 0.5 / sqrt(16384).
All inputs are finite; a program needn't handle non-finite values.
Results may differ from a plain program's by a relative error of at most 0.0048.
Values may be sent and summed in bfloat16 or wider, within the bound.
A program may use at most 32 MiB of HBM per device.

v0:
```python
import jax
import jax.numpy as jnp
from jax import lax
from jax.sharding import PartitionSpec as P

BLK_DEV = 1


def shards(valence, conduction, points, inverse_metric):
    interp_count = lax.axis_size("interp")
    points_dev = valence.shape[0]
    first_point = (lax.axis_index("grid") * interp_count + lax.axis_index("interp")) * points_dev
    offsets = points - first_point
    inside_mask = ((offsets >= 0) & (offsets < points_dev))[:, None]
    clipped = jnp.clip(offsets, 0, points_dev - 1)
    zero_value = jnp.zeros((), jnp.bfloat16)
    picked_val = jnp.where(inside_mask, jnp.take(valence, clipped, axis=0), zero_value)
    picked_con = jnp.where(inside_mask, jnp.take(conduction, clipped, axis=0), zero_value)
    summed_val, summed_con = (
        lax.psum(picked_val, "interp").astype(jnp.float32),
        lax.psum(picked_con, "interp").astype(jnp.float32),
    )
    point_val = summed_val.astype(jnp.bfloat16)
    point_con = summed_con.astype(jnp.bfloat16)
    width_val = valence.shape[1]
    block_pair = jnp.concatenate([valence[:BLK_DEV], conduction[:BLK_DEV]], axis=1)
    contract = (((1,), (1,)), ((), ()))
    block_rows = lax.all_gather(block_pair, ("grid", "interp"), axis=0, tiled=True)
    gram_val = lax.dot_general(
        block_rows[:, :width_val], point_val, contract, preferred_element_type=jnp.float32
    )
    gram_con = lax.dot_general(
        block_rows[:, width_val:], point_con, contract, preferred_element_type=jnp.float32
    )
    partial_value = jnp.dot(
        (gram_val * gram_con).astype(jnp.bfloat16),
        inverse_metric,
        preferred_element_type=jnp.float32,
    )
    return lax.psum_scatter(partial_value, "grid", scatter_dimension=0, tiled=True).astype(
        jnp.bfloat16
    )


def solution(mesh):
    return jax.shard_map(
        shards,
        mesh=mesh,
        in_specs=(
            P(("grid", "interp"), None),
            P(("grid", "interp"), None),
            P("grid"),
            P("grid", "interp"),
        ),
        out_specs=P("grid", "interp"),
        check_vma=False,
    )
```

profile of v0, /device:TPU:1, one launch (start us, length us, event | category | flops | bytes accessed | tf_op | source)
XLA Modules:
  0.0 1715.1 jit_solution(18381979393019317153)
XLA Ops:
  7.4 0.0 copy-start
  7.4 0.0 all-gather.3.cloned.1.call-start
  7.4 0.8 slice.12
  8.1 0.7 slice.13
  8.8 0.6 maximum_bitcast_fusion
  9.4 0.0 all-gather.3.cloned.1.call-update
  9.5 0.0 all-reduce.3.cloned.1.call-start
  9.5 0.7 compare_and_fusion
  10.2 0.0 copy-start.1
  10.2 3.0 gather_fusion.1
  13.2 0.0 copy-done.1
  13.3 2.0 gather_fusion
  15.2 1.2 select_select_fusion
  16.5 0.0 all-reduce.3.cloned.1.call-update
  16.5 0.0 reduce-scatter.2.cloned.1.call-start
  16.6 1541.6 %all-gather.3.cloned.1.call-done = bf16[1024,1,1024]{2,1,0:T(2,128)(2,1)} async-done(((bf16[1,1,1024]{2,1,0:T(2,128)(2,1)}), bf16[1024,1,1024]{2,1,0:T(2,128)(2,1)}) %all-gather.3.cloned.1.call-update) | async-done | bytes 2097168 | tf_op jit(solution)/shard_map/all_gather | solution.py:28
  1558.2 4.3 copy.7
  1562.5 0.0 all-reduce.3.cloned.1.call-done
  1562.5 0.0 copy-start.2
  1562.5 2.2 fusion.3
  1564.7 0.0 copy-done
  1564.7 0.0 copy-done.2
  1564.7 3.8 fusion
  1568.5 0.0 reduce-scatter.2.cloned.1.call-update
  1568.5 137.7 %reduce-scatter.2.cloned.1.call-done = f32[32,512]{1,0:T(8,128)} async-done(((f32[1024,512]{1,0:T(8,128)}), f32[32,512]{1,0:T(8,128)}) %reduce-scatter.2.cloned.1.call-update) | async-done | bytes 65552 | tf_op jit(solution)/shard_map/reduce_scatter | solution.py:40
  1706.2 1.5 convert_element_type.5
  (1 shorter events, 0.0 us)
Async XLA Ops:
  7.4 1557.3 %copy-start = (bf16[512,512]{1,0:T(8,128)(2,1)S(1)}, bf16[512,512]{1,0:T(8,128)(2,1)}, u32[]{:S(2)}) copy-start(bf16[512,512]{1,0:T(8,128)(2,1)} %param.9) | copy-start | bytes 1572868
  7.4 1550.8 %all-gather.3.cloned.1.call-start = ((), (), s32[]{:S(2)}) async-start(), calls=%async_computation.2 | async-start | bytes 4198400 | tf_op jit(solution)/shard_map/all_gather | solution.py:28
  9.5 1553.0 %all-reduce.3.cloned.1.call-start = ((), (), s32[]{:S(2)}) async-start(), calls=%async_computation.3 | async-start | bytes 2097152 | tf_op jit(solution)/shard_map/psum | solution.py:20
  10.2 3.0 copy-start.1
  16.5 1689.7 %reduce-scatter.2.cloned.1.call-start = ((), (), s32[]{:S(2)}) async-start(), calls=%async_computation.1 | async-start | bytes 2162688 | tf_op jit(solution)/shard_map/reduce_scatter | solution.py:40
  1562.5 2.2 copy-start.2
Sparse Core Ops, SparseCore 0:
  11.3 1546.7 all-gather.2
Sparse Core Ops, SparseCore 1:
  16.6 366.9 all-reduce.2
  1568.6 137.5 reduce-scatter.1
where the time goes:
time: 1740 us; the launch traced here: 1720 us
  waiting for transfers between devices  1680 us (97%)
    all_gather x1, waiting for transfers between devices, shards(): lax.all_gather(block_pair, ('grid', 'interp'), axis=0, tiled=True)  1540 us
    reduce_scatter x1, waiting for transfers between devices, shards(): lax.psum_scatter(partial_value, 'grid', scatter_dimension=0, tiled=True)  138 us
  transfers between devices with their start and end apart: 3, of which 2 were waited for; matrix products, arithmetic and copies ran while one was open for 1% of the time, Pallas kernels for 0%

commit v1 on v0

v1 whole, which is shorter than its diff:
```python
import jax
import jax.numpy as jnp
from jax import lax
from jax.experimental import pallas as pl
from jax.experimental.pallas import tpu as pltpu
from jax.sharding import PartitionSpec as P

MESH = pl.DeviceIdType.MESH
BF16, F32 = jnp.bfloat16, jnp.float32

NX, NZL, NY = 8, 4, 8
COPIES = 3 + 3 * (NY - 1) + (NZL - 1) + 3 * (NX - 1) + 3 + (NY - 1) + (2 * NZL - 1)


def kernel(
    pts_ref, val_ref, con_ref, met_ref, out_ref,
    val_mate, con_mate, met_mate, row_buf, zl_buf, blk_buf,
    pick_buf, pick_in, pick_z, pts_buf, pair_buf, part_buf, part_in, sum_buf, sum_in,
    send_sem, recv_sem,
):
    g, i = lax.axis_index("grid"), lax.axis_index("interp")
    x, zl = lax.div(g, NZL), lax.rem(g, NZL)
    y, zh, c = lax.div(i, 4), lax.rem(lax.div(i, 2), 2), lax.rem(i, 2)
    rows, width = val_ref.shape
    half = pts_ref.shape[1] // 2
    piece = half // NY
    mate = 1 - c

    def device(x=x, zl=zl, y=y, zh=zh, c=c):
        return (x * NZL + zl, y * 4 + zh * 2 + c)

    y_peers = [device(y=lax.rem(y + k, NY)) for k in range(1, NY)]
    x_peers = [device(x=lax.rem(x + k, NX)) for k in range(1, NX)]
    zl_peers = [device(zl=lax.rem(zl + k, NZL)) for k in range(1, NZL)]
    zl_mates = [device(zl=lax.rem(zl + k, NZL), c=mate) for k in range(1, NZL)]
    z_peer, core_peer = device(zh=1 - zh), device(c=mate)

    barrier = pltpu.get_barrier_semaphore()
    peers = [core_peer, z_peer] + y_peers + x_peers + zl_peers + zl_mates
    for peer in peers:
        pl.semaphore_signal(barrier, inc=1, device_id=peer, device_id_type=MESH)

    copies = []

    def send(src, dst, peer):
        n = len(copies)
        copy = pltpu.make_async_remote_copy(
            src_ref=src,
            dst_ref=dst,
            send_sem=send_sem.at[n],
            recv_sem=recv_sem.at[n],
            device_id=peer,
            device_id_type=MESH,
        )
        copy.start()
        copies.append(copy)
        return copy

    row_buf[y] = jnp.concatenate([val_ref[0:1, :], con_ref[0:1, :]], axis=1).astype(F32)

    pts = pts_ref[:, pl.ds(pl.multiple_of(c * half, half), half)]
    spread = jnp.broadcast_to(pts, (128, half)).T

    def picked(owner, val, con):
        local = spread - owner * rows
        lane = lax.broadcasted_iota(jnp.int32, (half, 128), 1)
        hot = jnp.concatenate(
            [jnp.where(local == lane + at, 1.0, 0.0) for at in range(0, rows, 128)], axis=1
        ).astype(BF16)
        return [
            jnp.dot(hot, ref[...], preferred_element_type=F32).astype(BF16).reshape(NY, piece, width)
            for ref in (val, con)
        ]

    own = g * (NY * 4) + i
    pick_val, pick_con = picked(own, val_ref, con_ref)
    pick_buf[:, :, :width] = pick_val
    pick_buf[:, :, width:] = pick_con

    pl.semaphore_wait(barrier, len(peers))

    core_rows = [send(val_ref, val_mate, core_peer), send(con_ref, con_mate, core_peer)]
    row_copies = [send(row_buf.at[y], row_buf.at[y], peer) for peer in y_peers]
    core_met = send(met_ref, met_mate, core_peer)

    for copy in core_rows:
        copy.wait_recv()
    pick_val, pick_con = picked(own - c + mate, val_mate, con_mate)
    pick_buf[:, :, :width] += pick_val
    pick_buf[:, :, width:] += pick_con
    pick_copies = [
        send(pick_buf.at[lax.rem(y + k, NY)], pick_in.at[k - 1], y_peers[k - 1])
        for k in range(1, NY)
    ]

    for copy in row_copies:
        copy.wait_recv()
    for k in range(NY):
        zl_buf[zl, k : k + 1, :] = row_buf[k]
    zl_copies = [send(zl_buf.at[zl], zl_buf.at[zl], peer) for peer in zl_peers]
    for copy in zl_copies:
        copy.wait_recv()
    blk_buf[x] = zl_buf[...].reshape(NZL * NY, 2 * width).astype(BF16)
    blk_copies = [send(blk_buf.at[x], blk_buf.at[x], peer) for peer in x_peers]

    for copy in pick_copies:
        copy.wait_recv()
    total = pick_buf[y].astype(F32)
    for k in range(NY - 1):
        total += pick_in[k].astype(F32)
    pts_buf[c] = total.astype(BF16)
    z_copy = send(pts_buf.at[c], pick_z, z_peer)
    z_copy.wait_recv()
    z_copy.wait_send()
    pts_buf[c] = (total + pick_z[...].astype(F32)).astype(BF16)
    core_copy = send(pts_buf.at[c], pts_buf.at[c], core_peer)
    core_copy.wait_recv()
    for copy in blk_copies:
        copy.wait_recv()

    block = blk_buf[...].reshape(NX * NZL * NY, 2 * width)
    points = pts_buf[...].reshape(2 * piece, 2 * width)
    across = (((1,), (1,)), ((), ()))
    gram_val = lax.dot_general(points[:, :width], block[:, :width], across, preferred_element_type=F32)
    gram_con = lax.dot_general(points[:, width:], block[:, width:], across, preferred_element_type=F32)
    pair = (gram_val * gram_con).astype(BF16)
    pair_buf[zh, :, y] = pair.reshape(2, piece, NX * NZL * NY)

    mine, theirs = pair_buf.at[zh, :, y], pair_buf.at[1 - zh, :, y]
    pair_z = send(mine, mine, z_peer)
    pair_copies = [send(mine, mine, peer) for peer in y_peers]
    pair_z.wait_recv()
    pair_copies += [send(theirs, theirs, peer) for peer in y_peers]
    core_met.wait_recv()
    for copy in pair_copies:
        copy.wait_recv()

    down = (((0,), (0,)), ((), ()))
    part_copies = []
    for metric, to_core in ((met_mate, mate), (met_ref, c)):
        for q in range(2):
            pair_q = pair_buf[q].reshape(2 * half, NX * NZL * NY)
            part = lax.dot_general(pair_q, metric[...], down, preferred_element_type=F32)
            part_buf[to_core, :, q] = part.astype(BF16).reshape(NX, NZL * NY, width)
        part_copies += [
            send(
                part_buf.at[to_core, lax.rem(x + k, NX)],
                part_in.at[k - 1, to_core],
                x_peers[k - 1],
            )
            for k in range(1, NX)
        ]
    for copy in part_copies:
        copy.wait_recv()

    for to_core in range(2):
        sums = []
        for q in range(2):
            s = part_buf[to_core, x, q].astype(F32)
            for k in range(NX - 1):
                s += part_in[k, to_core, q].astype(F32)
            sums.append(s)
        for to_zl in range(NZL):
            at = to_zl * NY
            sum_buf[to_zl, to_core] = jnp.concatenate(
                [s[at : at + NY] for s in sums], axis=0
            ).astype(BF16)
    sum_copies = []
    for k in range(NZL):
        for dc in range(2):
            if k or dc:
                to_zl = lax.rem(zl + k, NZL)
                to_core = mate if dc else c
                sum_copies.append(
                    send(sum_buf.at[to_zl, to_core], sum_in.at[k, c], device(zl=to_zl, c=to_core))
                )
    sum_in[0, c] = sum_buf[zl, c]
    for copy in sum_copies:
        copy.wait_recv()
    for from_core in range(2):
        s = sum_in[0, from_core].astype(F32)
        for k in range(1, NZL):
            s += sum_in[k, from_core].astype(F32)
        out_ref[from_core] = s.reshape(2, NY, width)

    for n, copy in enumerate(copies):
        if copy is not z_copy:
            copy.wait_send()


def shards(valence, conduction, points, inverse_metric):
    rows, width = valence.shape
    count = points.shape[0]
    piece = count // 2 // NY
    lines = NX * NZL * NY
    vmem = pl.BlockSpec(memory_space=pltpu.VMEM)
    out = pl.pallas_call(
        kernel,
        out_shape=jax.ShapeDtypeStruct((2, 2, NY, width), F32),
        in_specs=[vmem] * 4,
        out_specs=vmem,
        scratch_shapes=[
            pltpu.VMEM((rows, width), BF16),
            pltpu.VMEM((rows, width), BF16),
            pltpu.VMEM((count, width), BF16),
            pltpu.VMEM((NY, 1, 2 * width), F32),
            pltpu.VMEM((NZL, NY, 2 * width), F32),
            pltpu.VMEM((NX, NZL * NY, 2 * width), BF16),
            pltpu.VMEM((NY, piece, 2 * width), BF16),
            pltpu.VMEM((NY - 1, piece, 2 * width), BF16),
            pltpu.VMEM((piece, 2 * width), BF16),
            pltpu.VMEM((2, piece, 2 * width), BF16),
            pltpu.VMEM((2, 2, NY, piece, lines), BF16),
            pltpu.VMEM((2, NX, 2, NZL * NY, width), BF16),
            pltpu.VMEM((NX - 1, 2, 2, NZL * NY, width), BF16),
            pltpu.VMEM((NZL, 2, 2 * NY, width), BF16),
            pltpu.VMEM((NZL, 2, 2 * NY, width), BF16),
            pltpu.SemaphoreType.DMA((COPIES,)),
            pltpu.SemaphoreType.DMA((COPIES,)),
        ],
        compiler_params=pltpu.CompilerParams(
            collective_id=0, has_side_effects=True, vmem_limit_bytes=40 * 2**20
        ),
    )(points[None, :], valence, conduction, inverse_metric)
    return out.transpose(2, 1, 0, 3).reshape(NY * 4, width).astype(BF16)


def solution(mesh):
    return jax.shard_map(
        shards,
        mesh=mesh,
        in_specs=(
            P(("grid", "interp"), None),
            P(("grid", "interp"), None),
            P("grid"),
            P("grid", "interp"),
        ),
        out_specs=P("grid", "interp"),
        check_vma=False,
    )
```

time: 1740 us -> 97.2 us (0.06); the launches traced: 1720 us -> 96.9 us
  waiting for transfers between devices: 1680 us -> 0 us
  Pallas kernels: 0 us -> 92.6 us
    all_gather x1 -> x0, waiting for transfers between devices: 1540 us -> none  [shards(): lax.all_gather(block_pair, ('grid', 'interp'), axis=0, tiled=True)]
    reduce_scatter x1 -> x0, waiting for transfers between devices: 138 us -> none  [shards(): lax.psum_scatter(partial_value, 'grid', scatter_dimension=0, tiled=True)]
    pallas_call x0 -> x1, Pallas kernels: none -> 92.6 us  [shards(): pl.pallas_call(kernel, out_shape=jax.ShapeDtypeStruct((2, 2, NY, width),...]
  transfers between devices with their start and end apart: 3 -> 0, of which waited for: 2 -> 0; matrix products, arithmetic and copies ran while one was open for 1% -> 0% of each run, Pallas kernels for 0% -> 0%
where the time goes in v1:
time: 97.2 us; the launch traced here: 96.9 us
  Pallas kernels  92.6 us (95%)
  local copies, waits for them, and re-layouts  4.29 us (4%)
    pallas_call x1, Pallas kernels, shards(): pl.pallas_call(kernel, out_shape=jax.ShapeDtypeStruct((2, 2, NY, width),...  92.6 us
    unnamed x8, local copies, waits for them, and re-layouts  3.62 us

profile of v1, /device:TPU:1, one launch (start us, length us, event | category | flops | bytes accessed | tf_op | source)
XLA Modules:
  0.0 96.9 jit_solution(9861237559258967092)
XLA Ops:
  0.0 0.0 copy-start
  0.0 1.0 %copy-done = bf16[512,512]{1,0:T(8,128)(2,1)S(1)} copy-done((bf16[512,512]{1,0:T(8,128)(2,1)S(1)}, bf16[512,512]{1,0:T(8,128)(2,1)}, u32[]{:S(2)}) %copy-start) | copy-done | bytes 524312
  1.0 0.0 copy-start.1
  1.0 0.9 copy-done.1
  2.0 0.0 copy-start.2
  2.0 0.9 copy-done.2
  2.9 0.0 copy-start.3
  2.9 0.7 copy-done.3
  3.6 92.6 %shard_map.46 = f32[2,2,8,512]{3,2,1,0:T(8,128)S(1)} custom-call(s32[1,512]{1,0:T(1,128)S(1)} %bitcast.3, bf16[256,512]{1,0:T(8,128)(2,1)S(1)} %copy-done.1, bf16[256,512]{1,0:T(8,128)(2,1)S(1)} %copy-done.2, bf16[512,512]{1,0:T(8,128)(2,1)S(1)} %copy-done), custom_call_target="tpu_custom_call" | custom-call | tf_op jit(solution)/shard_map/pallas_call | solution.py:197
  96.3 0.6 convert_element_type.11
  (2 shorter events, 0.0 us)
Async XLA Ops:
  0.0 1.0 %copy-start = (bf16[512,512]{1,0:T(8,128)(2,1)S(1)}, bf16[512,512]{1,0:T(8,128)(2,1)}, u32[]{:S(2)}) copy-start(bf16[512,512]{1,0:T(8,128)(2,1)} %met_ref.1) | copy-start | bytes 1572868
  1.0 0.9 copy-start.1
  2.0 0.9 copy-start.2
  2.9 0.7 copy-start.3

commit v2 on v1

v2 whole, which is shorter than its diff:
```python
import jax
import jax.numpy as jnp
from jax import lax
from jax.experimental import pallas as pl
from jax.experimental.pallas import tpu as pltpu
from jax.sharding import PartitionSpec as P

MESH = pl.DeviceIdType.MESH
BF16, F32 = jnp.bfloat16, jnp.float32

NX, NZL, NY = 8, 4, 8
COPIES = 112


def kernel(
    pts_hbm, val_hbm, con_hbm, met_hbm, out_ref,
    pts_ref, val_ref, con_ref, met_ref, val_mate, con_mate, met_mate, row_buf, zl_buf, blk_buf,
    pick_buf, pick_in, pick_z, pts_buf, pair_buf,
    px_buf, px_in, pz_buf, pz_in, sx_buf, sx_in, sz_buf, sz_in,
    send_sem, recv_sem, load_sem,
):
    g, i = lax.axis_index("grid"), lax.axis_index("interp")
    x, zl = lax.div(g, NZL), lax.rem(g, NZL)
    y, zh, c = lax.div(i, 4), lax.rem(lax.div(i, 2), 2), lax.rem(i, 2)
    rows, width = val_ref.shape
    half = pts_ref.shape[1] // 2
    piece = half // NY
    lines = NX * NZL * NY
    mate = 1 - c

    def device(x=x, zl=zl, y=y, zh=zh, c=c):
        return (x * NZL + zl, y * 4 + zh * 2 + c)

    y_peers = [device(y=lax.rem(y + k, NY)) for k in range(1, NY)]
    x_peers = [device(x=lax.rem(x + k, NX)) for k in range(1, NX)]
    zl_peers = [device(zl=lax.rem(zl + k, NZL)) for k in range(1, NZL)]
    zl_mates = [device(zl=lax.rem(zl + k, NZL), c=mate) for k in range(1, NZL)]
    z_peer, core_peer = device(zh=1 - zh), device(c=mate)

    barrier = pltpu.get_barrier_semaphore()
    peers = [core_peer, z_peer] + x_peers + y_peers + zl_peers + zl_mates
    for peer in peers:
        pl.semaphore_signal(barrier, inc=1, device_id=peer, device_id_type=MESH)

    loads = [
        pltpu.make_async_copy(src, dst, load_sem.at[n])
        for n, (src, dst) in enumerate(
            [(val_hbm, val_ref), (con_hbm, con_ref), (pts_hbm, pts_ref), (met_hbm, met_ref)]
        )
    ]
    for load in loads:
        load.start()

    copies = []

    def send(src, dst, peer):
        n = len(copies)
        copy = pltpu.make_async_remote_copy(
            src_ref=src,
            dst_ref=dst,
            send_sem=send_sem.at[n],
            recv_sem=recv_sem.at[n],
            device_id=peer,
            device_id_type=MESH,
        )
        copy.start()
        copies.append(copy)
        return copy

    for load in loads[:2]:
        load.wait()
    row_buf[y] = jnp.concatenate([val_ref[0:1, :], con_ref[0:1, :]], axis=1).astype(F32)

    pl.semaphore_wait(barrier, len(peers))

    row_copies = [send(row_buf.at[y], row_buf.at[y], peer) for peer in y_peers]
    core_rows = [send(val_ref, val_mate, core_peer), send(con_ref, con_mate, core_peer)]

    loads[2].wait()
    pts = pts_ref[:, pl.ds(pl.multiple_of(c * half, half), half)]
    spread = jnp.broadcast_to(pts, (128, half)).T

    def one_hot(owner):
        local = spread - owner * rows
        lane = lax.broadcasted_iota(jnp.int32, (half, 128), 1)
        return jnp.concatenate(
            [jnp.where(local == lane + at, 1.0, 0.0) for at in range(0, rows, 128)], axis=1
        ).astype(BF16)

    def picked(hot, ref):
        pick = jnp.dot(hot, ref[...], preferred_element_type=F32)
        return pick.astype(BF16).reshape(NY, piece, width)

    own = g * (NY * 4) + i
    hot, hot_mate = one_hot(own), one_hot(own - c + mate)

    for h, ref in enumerate((val_ref, con_ref)):
        pick_buf[h] = picked(hot, ref)
    pick_copies = []
    for h, ref in enumerate((val_mate, con_mate)):
        core_rows[h].wait_recv()
        pick_buf[h] += picked(hot_mate, ref)
        pick_copies.append([
            send(pick_buf.at[h, lax.rem(y + k, NY)], pick_in.at[h, k - 1], y_peers[k - 1])
            for k in range(1, NY)
        ])

    for copy in row_copies:
        copy.wait_recv()
    for k in range(NY):
        zl_buf[zl, k : k + 1, :] = row_buf[k]
    zl_copies = [send(zl_buf.at[zl], zl_buf.at[zl], peer) for peer in zl_peers]

    for copy in zl_copies:
        copy.wait_recv()
    blk_buf[x] = zl_buf[...].reshape(2, NZL * NY // 2, 2 * width).astype(BF16)
    blk_copies = [send(blk_buf.at[x], blk_buf.at[x], peer) for peer in x_peers]
    loads[3].wait()
    core_met = send(met_ref, met_mate, core_peer)

    z_copies = []
    for h in range(2):
        for copy in pick_copies[h]:
            copy.wait_recv()
        total = pick_buf[h, y].astype(F32)
        for k in range(NY - 1):
            total += pick_in[h, k].astype(F32)
        pts_buf[h, 0] = total.astype(BF16)
        z_copies.append(send(pts_buf.at[h, 0], pick_z.at[h], z_peer))
    core_copies = []
    for h in range(2):
        z_copies[h].wait_recv()
        pts_buf[h, 1 + c] = (pts_buf[h, 0].astype(F32) + pick_z[h].astype(F32)).astype(BF16)
        core_copies.append(send(pts_buf.at[h, 1 + c], pts_buf.at[h, 1 + c], core_peer))
    for copy in blk_copies:
        copy.wait_recv()

    across = (((1,), (1,)), ((), ()))
    block = blk_buf[...].reshape(lines, 2 * width)
    grams = []
    for h in range(2):
        core_copies[h].wait_recv()
        points = pts_buf[h, 1:].reshape(2 * piece, width)
        grams.append(
            lax.dot_general(
                points, block[:, h * width : (h + 1) * width], across, preferred_element_type=F32
            )
        )
    pair_buf[0, :, y] = (grams[0] * grams[1]).astype(BF16).reshape(2, piece, lines)

    mine, theirs = pair_buf.at[0, :, y], pair_buf.at[1, :, y]
    pair_z = send(mine, theirs, z_peer)
    pair_copies = [send(mine, mine, peer) for peer in y_peers]
    pair_z.wait_recv()
    pair_copies += [send(theirs, theirs, peer) for peer in y_peers]
    for copy in pair_copies:
        copy.wait_recv()
    core_met.wait_recv()

    down = (((0,), (0,)), ((), ()))

    def share(q, metric):
        pair_q = pair_buf[q].reshape(2 * half, lines)
        return lax.dot_general(pair_q, metric[...], down, preferred_element_type=F32)

    for q in range(2):
        part = share(q, met_mate)
        px_buf[:, q] = part.astype(BF16).reshape(NX, NZL * NY, width)
    px_copies = [
        send(px_buf.at[lax.rem(x + k, NX)], px_in.at[k - 1], x_peers[k - 1]) for k in range(1, NX)
    ]
    for q in range(2):
        part = share(q, met_ref).reshape(NX, NZL, NY, width)
        for k in range(NZL):
            pz_buf[k, q] = part[:, k].reshape(NX * NY, width).astype(BF16)
    pz_copies = [
        send(pz_buf.at[lax.rem(zl + k, NZL)], pz_in.at[k - 1], zl_peers[k - 1])
        for k in range(1, NZL)
    ]

    def summed(own, inbox, count):
        total = own.astype(F32)
        for k in range(count):
            total += inbox(k).astype(F32)
        return total

    for copy in pz_copies:
        copy.wait_recv()
    sums = [summed(pz_buf[zl, q], lambda k: pz_in[k, q], NZL - 1) for q in range(2)]
    for k in range(NX):
        sx_buf[k] = jnp.concatenate([s[k * NY : (k + 1) * NY] for s in sums], axis=0).astype(BF16)
    sx_copies = [
        send(sx_buf.at[lax.rem(x + k, NX)], sx_in.at[k - 1], x_peers[k - 1]) for k in range(1, NX)
    ]
    for copy in px_copies:
        copy.wait_recv()
    sums = [summed(px_buf[x, q], lambda k: px_in[k, q], NX - 1) for q in range(2)]
    for k in range(NZL):
        sz_buf[k] = jnp.concatenate([s[k * NY : (k + 1) * NY] for s in sums], axis=0).astype(BF16)
    sz_copies = [
        send(sz_buf.at[lax.rem(zl + k, NZL)], sz_in.at[k], device(zl=lax.rem(zl + k, NZL), c=mate))
        for k in range(NZL)
    ]
    for copy in sx_copies:
        copy.wait_recv()
    s = summed(sx_buf[x], lambda k: sx_in[k], NX - 1)
    out_ref[c, zh], out_ref[c, 1 - zh] = s[:NY], s[NY:]
    for copy in sz_copies:
        copy.wait_recv()
    s = summed(sz_in[0], lambda k: sz_in[k + 1], NZL - 1)
    out_ref[mate, zh], out_ref[mate, 1 - zh] = s[:NY], s[NY:]

    for copy in copies:
        copy.wait_send()


def shards(valence, conduction, points, inverse_metric):
    rows, width = valence.shape
    count = points.shape[0]
    piece = count // 2 // NY
    lines = NX * NZL * NY
    out = pl.pallas_call(
        kernel,
        out_shape=jax.ShapeDtypeStruct((2, 2, NY, width), F32),
        in_specs=[pl.BlockSpec(memory_space=pltpu.HBM)] * 4,
        out_specs=pl.BlockSpec(memory_space=pltpu.VMEM),
        scratch_shapes=[
            pltpu.VMEM((1, count), jnp.int32),
            pltpu.VMEM((rows, width), BF16),
            pltpu.VMEM((rows, width), BF16),
            pltpu.VMEM((count, width), BF16),
            pltpu.VMEM((rows, width), BF16),
            pltpu.VMEM((rows, width), BF16),
            pltpu.VMEM((count, width), BF16),
            pltpu.VMEM((NY, 1, 2 * width), F32),
            pltpu.VMEM((NZL, NY, 2 * width), F32),
            pltpu.VMEM((NX, 2, NZL * NY // 2, 2 * width), BF16),
            pltpu.VMEM((2, NY, piece, width), BF16),
            pltpu.VMEM((2, NY - 1, piece, width), BF16),
            pltpu.VMEM((2, piece, width), BF16),
            pltpu.VMEM((2, 3, piece, width), BF16),
            pltpu.VMEM((2, 2, NY, piece, lines), BF16),
            pltpu.VMEM((NX, 2, NZL * NY, width), BF16),
            pltpu.VMEM((NX - 1, 2, NZL * NY, width), BF16),
            pltpu.VMEM((NZL, 2, NX * NY, width), BF16),
            pltpu.VMEM((NZL - 1, 2, NX * NY, width), BF16),
            pltpu.VMEM((NX, 2 * NY, width), BF16),
            pltpu.VMEM((NX - 1, 2 * NY, width), BF16),
            pltpu.VMEM((NZL, 2 * NY, width), BF16),
            pltpu.VMEM((NZL, 2 * NY, width), BF16),
            pltpu.SemaphoreType.DMA((COPIES,)),
            pltpu.SemaphoreType.DMA((COPIES,)),
            pltpu.SemaphoreType.DMA((4,)),
        ],
        compiler_params=pltpu.CompilerParams(
            collective_id=0, has_side_effects=True, vmem_limit_bytes=63 * 2**20
        ),
    )(points[None, :], valence, conduction, inverse_metric)
    return out.transpose(2, 1, 0, 3).reshape(NY * 4, width).astype(BF16)


def solution(mesh):
    return jax.shard_map(
        shards,
        mesh=mesh,
        in_specs=(
            P(("grid", "interp"), None),
            P(("grid", "interp"), None),
            P("grid"),
            P("grid", "interp"),
        ),
        out_specs=P("grid", "interp"),
        check_vma=False,
    )
```

time: 97.2 us -> 82.5 us (0.85)
  Pallas kernels: 92.6 us -> 80.8 us
  local copies, waits for them, and re-layouts: 4.29 us -> 0.67 us
    pallas_call x1, Pallas kernels: 92.6 us -> 80.8 us  [shards(): pl.pallas_call(kernel, out_shape=jax.ShapeDtypeStruct((2, 2, NY, width),...]
    unnamed x8 -> x0, local copies, waits for them, and re-layouts: 3.62 us -> none
where the time goes in v2:
time: 82.5 us; the launch traced here: 82.3 us
  Pallas kernels  80.8 us (98%)
  other arithmetic  0.85 us (1%)
    pallas_call x1, Pallas kernels, shards(): pl.pallas_call(kernel, out_shape=jax.ShapeDtypeStruct((2, 2, NY, width),...  80.8 us

profile of v2, /device:TPU:1, one launch (start us, length us, event | category | flops | bytes accessed | tf_op | source)
XLA Modules:
  0.0 82.3 jit_solution(6556976963178835448)
XLA Ops:
  0.0 80.8 %shard_map.46 = f32[2,2,8,512]{3,2,1,0:T(8,128)} custom-call(s32[1,512]{1,0:T(1,128)} %bitcast.3, bf16[256,512]{1,0:T(8,128)(2,1)} %val_hbm.1, bf16[256,512]{1,0:T(8,128)(2,1)} %con_hbm.1, bf16[512,512]{1,0:T(8,128)(2,1)} %met_hbm.1), custom_call_target="tpu_custom_call" | custom-call | tf_op jit(solution)/shard_map/pallas_call | solution.py:222
  80.8 0.8 %convert_bitcast_fusion = bf16[8,2,2,512]{3,0,1,2:T(8,128)(2,1)S(1)} fusion(f32[2,2,8,512]{3,2,1,0:T(8,128)} %shard_map.46), kind=kLoop, calls=%fused_computation | loop fusion | flops 16384 | bytes 98304 | tf_op jit(solution)/shard_map/convert_element_type | solution.py:259
  81.7 0.6 convert_element_type.11
  (1 shorter events, 0.0 us)

commit v3 on v2

--- a/solution.py
+++ b/solution.py
@@ -16,8 +16,8 @@
     pts_hbm, val_hbm, con_hbm, met_hbm, out_ref,
     pts_ref, val_ref, con_ref, met_ref, val_mate, con_mate, met_mate, row_buf, zl_buf, blk_buf,
     pick_buf, pick_in, pick_z, pts_buf, pair_buf,
-    px_buf, px_in, pz_buf, pz_in, sx_buf, sx_in, sz_buf, sz_in,
-    send_sem, recv_sem, load_sem,
+    part_buf, px_buf, px_in, pz_buf, pz_in, lx_buf, lx_in, lz_buf, lz_in, sx_buf, sx_in, sz_buf, sz_in,
+    send_sem, recv_sem, load_sem, rest_send, rest_recv,
 ):
     g, i = lax.axis_index("grid"), lax.axis_index("interp")
     x, zl = lax.div(g, NZL), lax.rem(g, NZL)
@@ -89,21 +89,25 @@
 
     def picked(hot, ref):
         pick = jnp.dot(hot, ref[...], preferred_element_type=F32)
-        return pick.astype(BF16).reshape(NY, piece, width)
+        return pick.astype(BF16).reshape(NY, 2, piece // 2, width)
 
     own = g * (NY * 4) + i
     hot, hot_mate = one_hot(own), one_hot(own - c + mate)
 
-    for h, ref in enumerate((val_ref, con_ref)):
-        pick_buf[h] = picked(hot, ref)
-    pick_copies = []
-    for h, ref in enumerate((val_mate, con_mate)):
-        core_rows[h].wait_recv()
-        pick_buf[h] += picked(hot_mate, ref)
-        pick_copies.append([
+    sides = (slice(0, width), slice(width, 2 * width))
+    picks = [picked(hot, ref) for ref in (val_ref, con_ref)]
+    for n, ref in enumerate((val_mate, con_mate)):
+        core_rows[n].wait_recv()
+        pick = picks[n] + picked(hot_mate, ref)
+        for h in range(2):
+            pick_buf[h, :, :, sides[n]] = pick[:, h]
+    pick_copies = [
+        [
             send(pick_buf.at[h, lax.rem(y + k, NY)], pick_in.at[h, k - 1], y_peers[k - 1])
             for k in range(1, NY)
-        ])
+        ]
+        for h in range(2)
+    ]
 
     for copy in row_copies:
         copy.wait_recv()
@@ -127,56 +131,108 @@
             total += pick_in[h, k].astype(F32)
         pts_buf[h, 0] = total.astype(BF16)
         z_copies.append(send(pts_buf.at[h, 0], pick_z.at[h], z_peer))
-    core_copies = []
+    across = (((1,), (1,)), ((), ()))
+    pair_z, pair_copies = [], [[], []]
     for h in range(2):
         z_copies[h].wait_recv()
         pts_buf[h, 1 + c] = (pts_buf[h, 0].astype(F32) + pick_z[h].astype(F32)).astype(BF16)
-        core_copies.append(send(pts_buf.at[h, 1 + c], pts_buf.at[h, 1 + c], core_peer))
-    for copy in blk_copies:
-        copy.wait_recv()
-
-    across = (((1,), (1,)), ((), ()))
-    block = blk_buf[...].reshape(lines, 2 * width)
-    grams = []
+        core_copy = send(pts_buf.at[h, 1 + c], pts_buf.at[h, 1 + c], core_peer)
+        if h == 0:
+            for copy in blk_copies:
+                copy.wait_recv()
+        core_copy.wait_recv()
+        points = pts_buf[h, 1:].reshape(piece, 2 * width)
+        grams = [
+            lax.dot_general(
+                points[:, side], blk_buf[...].reshape(lines, 2 * width)[:, side], across,
+                preferred_element_type=F32,
+            )
+            for side in sides
+        ]
+        pair = (grams[0] * grams[1]).astype(BF16)
+        pair_buf[0, :, y, h] = pair.reshape(2, piece // 2, lines)
+        mine, theirs = pair_buf.at[0, :, y, h], pair_buf.at[1, :, y, h]
+        pair_z.append(send(mine, theirs, z_peer))
+        pair_copies[0] += [send(mine, mine, peer) for peer in y_peers]
     for h in range(2):
-        core_copies[h].wait_recv()
-        points = pts_buf[h, 1:].reshape(2 * piece, width)
-        grams.append(
-            lax.dot_general(
-                points, block[:, h * width : (h + 1) * width], across, preferred_element_type=F32
-            )
+        pair_z[h].wait_recv()
+        theirs = pair_buf.at[1, :, y, h]
+        pair_copies[1] += [send(theirs, theirs, peer) for peer in y_peers]
+    core_met.wait_recv()
+
+    down = (((0,), (0,)), ((), ()))
+    i_mate = i - c + mate
+    x_from, zl_from = lax.div(i_mate, NZL), lax.rem(i, NZL)
+    x_line = (lax.rem(i_mate, NZL) == zl) & (x_from < NX)
+    zl_line = lax.div(i, NZL) == x
+    rest_x = dict(
+        n=0, src=x_line & (x_from == x), dst=x_line & (x_from != x), peers=x_peers, pos=x, size=NX,
+        hold=lx_buf, inbox=lx_in,
+    )
+    rest_z = dict(
+        n=1, src=zl_line & (zl_from == zl), dst=zl_line & (zl_from != zl), peers=zl_peers, pos=zl, size=NZL,
+        hold=lz_buf, inbox=lz_in,
+    )
+
+    def rest_copy(rest, q, k):
+        return pltpu.make_async_remote_copy(
+            src_ref=rest["hold"].at[q, lax.rem(rest["pos"] + k, rest["size"])],
+            dst_ref=rest["inbox"].at[q],
+            send_sem=rest_send.at[rest["n"], q, k - 1],
+            recv_sem=rest_recv.at[rest["n"], q],
+            device_id=rest["peers"][k - 1],
+            device_id_type=MESH,
         )
-    pair_buf[0, :, y] = (grams[0] * grams[1]).astype(BF16).reshape(2, piece, lines)
-
-    mine, theirs = pair_buf.at[0, :, y], pair_buf.at[1, :, y]
-    pair_z = send(mine, theirs, z_peer)
-    pair_copies = [send(mine, mine, peer) for peer in y_peers]
-    pair_z.wait_recv()
-    pair_copies += [send(theirs, theirs, peer) for peer in y_peers]
-    for copy in pair_copies:
-        copy.wait_recv()
-    core_met.wait_recv()
-
-    down = (((0,), (0,)), ((), ()))
-
-    def share(q, metric):
+
+    def send_rest(rest, q):
+        for k in range(1, rest["size"]):
+            rest_copy(rest, q, k).start()
+
+    def add_rest(rest, q, total):
+        @pl.when(rest["src"])
+        def _():
+            total[q] += rest["hold"][q, rest["pos"]].astype(F32).reshape(total.shape[1:])
+
+        if rest["size"] > 1:
+
+            @pl.when(rest["dst"])
+            def _():
+                rest_copy(rest, q, 1).wait_recv()
+                total[q] += rest["inbox"][q].astype(F32).reshape(total.shape[1:])
+
+    px_copies, pz_copies = [], []
+    for q in range(2):
+        for copy in pair_copies[q]:
+            copy.wait_recv()
         pair_q = pair_buf[q].reshape(2 * half, lines)
-        return lax.dot_general(pair_q, metric[...], down, preferred_element_type=F32)
-
-    for q in range(2):
-        part = share(q, met_mate)
-        px_buf[:, q] = part.astype(BF16).reshape(NX, NZL * NY, width)
-    px_copies = [
-        send(px_buf.at[lax.rem(x + k, NX)], px_in.at[k - 1], x_peers[k - 1]) for k in range(1, NX)
-    ]
-    for q in range(2):
-        part = share(q, met_ref).reshape(NX, NZL, NY, width)
+        part_buf[...] = lax.dot_general(pair_q, met_mate[...], down, preferred_element_type=F32)
+        px_buf[q] = part_buf[...].astype(BF16).reshape(NX, NZL * NY, width)
+        px_copies.append([
+            send(px_buf.at[q, lax.rem(x + k, NX)], px_in.at[q, k - 1], x_peers[k - 1])
+            for k in range(1, NX)
+        ])
+
+        @pl.when(rest_x["src"])
+        def _():
+            part = part_buf[...].reshape(NX, NZL * NY, width)
+            lx_buf[q] = (part - px_buf[q].astype(F32)).astype(BF16)
+            send_rest(rest_x, q)
+
+        part_buf[...] = lax.dot_general(pair_q, met_ref[...], down, preferred_element_type=F32)
         for k in range(NZL):
-            pz_buf[k, q] = part[:, k].reshape(NX * NY, width).astype(BF16)
-    pz_copies = [
-        send(pz_buf.at[lax.rem(zl + k, NZL)], pz_in.at[k - 1], zl_peers[k - 1])
-        for k in range(1, NZL)
-    ]
+            part = part_buf[...].reshape(NX, NZL, NY, width)[:, k]
+            pz_buf[q, k] = part.reshape(NX * NY, width).astype(BF16)
+        pz_copies.append([
+            send(pz_buf.at[q, lax.rem(zl + k, NZL)], pz_in.at[q, k - 1], zl_peers[k - 1])
+            for k in range(1, NZL)
+        ])
+
+        @pl.when(rest_z["src"])
+        def _():
+            for k in range(NZL):
+                part = part_buf[...].reshape(NX, NZL, NY, width)[:, k].reshape(NX * NY, width)
+                lz_buf[q, k] = (part - pz_buf[q, k].astype(F32)).astype(BF16)
+            send_rest(rest_z, q)
 
     def summed(own, inbox, count):
         total = own.astype(F32)
@@ -184,31 +240,42 @@
             total += inbox(k).astype(F32)
         return total
 
-    for copy in pz_copies:
-        copy.wait_recv()
-    sums = [summed(pz_buf[zl, q], lambda k: pz_in[k, q], NZL - 1) for q in range(2)]
-    for k in range(NX):
-        sx_buf[k] = jnp.concatenate([s[k * NY : (k + 1) * NY] for s in sums], axis=0).astype(BF16)
-    sx_copies = [
-        send(sx_buf.at[lax.rem(x + k, NX)], sx_in.at[k - 1], x_peers[k - 1]) for k in range(1, NX)
-    ]
-    for copy in px_copies:
-        copy.wait_recv()
-    sums = [summed(px_buf[x, q], lambda k: px_in[k, q], NX - 1) for q in range(2)]
+    for q in range(2):
+        for copy in pz_copies[q]:
+            copy.wait_recv()
+        total = summed(pz_buf[q, zl], lambda k: pz_in[q, k], NZL - 1)
+        sx_buf[q] = total.reshape(NX, NY, width)
+        add_rest(rest_z, q, sx_buf)
+        if q == 1:
+            sx_copies = [
+                send(sx_buf.at[:, lax.rem(x + k, NX)], sx_in.at[k - 1], x_peers[k - 1])
+                for k in range(1, NX)
+            ]
+        for copy in px_copies[q]:
+            copy.wait_recv()
+        total = summed(px_buf[q, x], lambda k: px_in[q, k], NX - 1)
+        sz_buf[q] = total.reshape(NZL, NY, width)
+        add_rest(rest_x, q, sz_buf)
+    sz_copies = []
     for k in range(NZL):
-        sz_buf[k] = jnp.concatenate([s[k * NY : (k + 1) * NY] for s in sums], axis=0).astype(BF16)
-    sz_copies = [
-        send(sz_buf.at[lax.rem(zl + k, NZL)], sz_in.at[k], device(zl=lax.rem(zl + k, NZL), c=mate))
-        for k in range(NZL)
-    ]
+        to_zl = lax.rem(zl + k, NZL)
+        sz_copies.append(send(sz_buf.at[:, to_zl], sz_in.at[k], device(zl=to_zl, c=mate)))
     for copy in sx_copies:
         copy.wait_recv()
-    s = summed(sx_buf[x], lambda k: sx_in[k], NX - 1)
-    out_ref[c, zh], out_ref[c, 1 - zh] = s[:NY], s[NY:]
+    total = summed(sx_buf[:, x], lambda k: sx_in[k], NX - 1)
+    out_ref[c, zh], out_ref[c, 1 - zh] = total[0], total[1]
     for copy in sz_copies:
         copy.wait_recv()
-    s = summed(sz_in[0], lambda k: sz_in[k + 1], NZL - 1)
-    out_ref[mate, zh], out_ref[mate, 1 - zh] = s[:NY], s[NY:]
+    total = summed(sz_in[0], lambda k: sz_in[k + 1], NZL - 1)
+    out_ref[mate, zh], out_ref[mate, 1 - zh] = total[0], total[1]
+
+    for rest in (rest_x, rest_z):
+
+        @pl.when(rest["src"])
+        def _():
+            for q in range(2):
+                for k in range(1, rest["size"]):
+                    rest_copy(rest, q, k).wait_send()
 
     for copy in copies:
         copy.wait_send()
@@ -235,22 +302,29 @@
             pltpu.VMEM((NY, 1, 2 * width), F32),
             pltpu.VMEM((NZL, NY, 2 * width), F32),
             pltpu.VMEM((NX, 2, NZL * NY // 2, 2 * width), BF16),
-            pltpu.VMEM((2, NY, piece, width), BF16),
-            pltpu.VMEM((2, NY - 1, piece, width), BF16),
-            pltpu.VMEM((2, piece, width), BF16),
-            pltpu.VMEM((2, 3, piece, width), BF16),
-            pltpu.VMEM((2, 2, NY, piece, lines), BF16),
-            pltpu.VMEM((NX, 2, NZL * NY, width), BF16),
-            pltpu.VMEM((NX - 1, 2, NZL * NY, width), BF16),
-            pltpu.VMEM((NZL, 2, NX * NY, width), BF16),
-            pltpu.VMEM((NZL - 1, 2, NX * NY, width), BF16),
-            pltpu.VMEM((NX, 2 * NY, width), BF16),
-            pltpu.VMEM((NX - 1, 2 * NY, width), BF16),
-            pltpu.VMEM((NZL, 2 * NY, width), BF16),
-            pltpu.VMEM((NZL, 2 * NY, width), BF16),
+            pltpu.VMEM((2, NY, piece // 2, 2 * width), BF16),
+            pltpu.VMEM((2, NY - 1, piece // 2, 2 * width), BF16),
+            pltpu.VMEM((2, piece // 2, 2 * width), BF16),
+            pltpu.VMEM((2, 3, piece // 2, 2 * width), BF16),
+            pltpu.VMEM((2, 2, NY, 2, piece // 2, lines), BF16),
+            pltpu.VMEM((lines, width), F32),
+            pltpu.VMEM((2, NX, NZL * NY, width), BF16),
+            pltpu.VMEM((2, NX - 1, NZL * NY, width), BF16),
+            pltpu.VMEM((2, NZL, NX * NY, width), BF16),
+            pltpu.VMEM((2, NZL - 1, NX * NY, width), BF16),
+            pltpu.VMEM((2, NX, NZL * NY, width), BF16),
+            pltpu.VMEM((2, NZL * NY, width), BF16),
+            pltpu.VMEM((2, NZL, NX * NY, width), BF16),
+            pltpu.VMEM((2, NX * NY, width), BF16),
+            pltpu.VMEM((2, NX, NY, width), F32),
+            pltpu.VMEM((NX - 1, 2, NY, width), F32),
+            pltpu.VMEM((2, NZL, NY, width), F32),
+            pltpu.VMEM((NZL, 2, NY, width), F32),
             pltpu.SemaphoreType.DMA((COPIES,)),
             pltpu.SemaphoreType.DMA((COPIES,)),
             pltpu.SemaphoreType.DMA((4,)),
+            pltpu.SemaphoreType.DMA((2, 2, NX - 1)),
+            pltpu.SemaphoreType.DMA((2, 2)),
         ],
         compiler_params=pltpu.CompilerParams(
             collective_id=0, has_side_effects=True, vmem_limit_bytes=63 * 2**20

time: 82.5 us -> 81.1 us (0.983)
  Pallas kernels: 80.8 us -> 79.4 us
    pallas_call x1, Pallas kernels: 80.8 us -> 79.4 us  [shards(): pl.pallas_call(kernel, out_shape=jax.ShapeDtypeStruct((2, 2, NY, width),...]
where the time goes in v3:
time: 81.1 us; the launch traced here: 80.9 us
  Pallas kernels  79.4 us (98%)
  other arithmetic  0.85 us (1%)
    pallas_call x1, Pallas kernels, shards(): pl.pallas_call(kernel, out_shape=jax.ShapeDtypeStruct((2, 2, NY, width),...  79.4 us

profile of v3, /device:TPU:1, one launch (start us, length us, event | category | flops | bytes accessed | tf_op | source)
XLA Modules:
  0.0 80.9 jit_solution(51262823185631501)
XLA Ops:
  0.0 79.4 %shard_map.46 = f32[2,2,8,512]{3,2,1,0:T(8,128)} custom-call(s32[1,512]{1,0:T(1,128)} %bitcast.3, bf16[256,512]{1,0:T(8,128)(2,1)} %val_hbm.1, bf16[256,512]{1,0:T(8,128)(2,1)} %con_hbm.1, bf16[512,512]{1,0:T(8,128)(2,1)} %met_hbm.1), custom_call_target="tpu_custom_call" | custom-call | tf_op jit(solution)/shard_map/pallas_call | solution.py:289
  79.4 0.8 %convert_bitcast_fusion = bf16[8,2,2,512]{3,0,1,2:T(8,128)(2,1)S(1)} fusion(f32[2,2,8,512]{3,2,1,0:T(8,128)} %shard_map.46), kind=kLoop, calls=%fused_computation | loop fusion | flops 16384 | bytes 98304 | tf_op jit(solution)/shard_map/convert_element_type | solution.py:333
  80.3 0.6 convert_element_type.11
  (1 shorter events, 0.0 us)

commit v4 on v3

--- a/solution.py
+++ b/solution.py
@@ -16,8 +16,8 @@
     pts_hbm, val_hbm, con_hbm, met_hbm, out_ref,
     pts_ref, val_ref, con_ref, met_ref, val_mate, con_mate, met_mate, row_buf, zl_buf, blk_buf,
     pick_buf, pick_in, pick_z, pts_buf, pair_buf,
-    part_buf, px_buf, px_in, pz_buf, pz_in, lx_buf, lx_in, lz_buf, lz_in, sx_buf, sx_in, sz_buf, sz_in,
-    send_sem, recv_sem, load_sem, rest_send, rest_recv,
+    part_buf, px_buf, px_in, pz_buf, pz_in, low_part, low_in, sx_buf, sx_in, sz_buf, sz_in,
+    send_sem, recv_sem, load_sem, low_send, low_recv,
 ):
     g, i = lax.axis_index("grid"), lax.axis_index("interp")
     x, zl = lax.div(g, NZL), lax.rem(g, NZL)
@@ -161,44 +161,33 @@
     core_met.wait_recv()
 
     down = (((0,), (0,)), ((), ()))
-    i_mate = i - c + mate
-    x_from, zl_from = lax.div(i_mate, NZL), lax.rem(i, NZL)
-    x_line = (lax.rem(i_mate, NZL) == zl) & (x_from < NX)
-    zl_line = lax.div(i, NZL) == x
-    rest_x = dict(
-        n=0, src=x_line & (x_from == x), dst=x_line & (x_from != x), peers=x_peers, pos=x, size=NX,
-        hold=lx_buf, inbox=lx_in,
-    )
-    rest_z = dict(
-        n=1, src=zl_line & (zl_from == zl), dst=zl_line & (zl_from != zl), peers=zl_peers, pos=zl, size=NZL,
-        hold=lz_buf, inbox=lz_in,
-    )
-
-    def rest_copy(rest, q, k):
+    lead, lead_mate = g == i, g == i - c + mate
+    side = width // 2
+
+    def low_copy(role, q, kx, kz):
+        to_x, to_zl = lax.rem(x + kx, NX), lax.rem(zl + kz, NZL)
         return pltpu.make_async_remote_copy(
-            src_ref=rest["hold"].at[q, lax.rem(rest["pos"] + k, rest["size"])],
-            dst_ref=rest["inbox"].at[q],
-            send_sem=rest_send.at[rest["n"], q, k - 1],
-            recv_sem=rest_recv.at[rest["n"], q],
-            device_id=rest["peers"][k - 1],
+            src_ref=low_part.at[q, to_x, to_zl],
+            dst_ref=low_in.at[role, q],
+            send_sem=low_send.at[q, kx * NZL + kz],
+            recv_sem=low_recv.at[role, q],
+            device_id=device(x=to_x, zl=to_zl, c=mate if role else c),
             device_id_type=MESH,
         )
 
-    def send_rest(rest, q):
-        for k in range(1, rest["size"]):
-            rest_copy(rest, q, k).start()
-
-    def add_rest(rest, q, total):
-        @pl.when(rest["src"])
-        def _():
-            total[q] += rest["hold"][q, rest["pos"]].astype(F32).reshape(total.shape[1:])
-
-        if rest["size"] > 1:
-
-            @pl.when(rest["dst"])
-            def _():
-                rest_copy(rest, q, 1).wait_recv()
-                total[q] += rest["inbox"][q].astype(F32).reshape(total.shape[1:])
+    def low_copies(role, q):
+        at = [(kx, kz) for kx in range(NX) for kz in range(NZL) if kx or kz or role]
+        return [low_copy(role, q, kx, kz) for kx, kz in at]
+
+    def keep_low(q, rounded):
+        part = part_buf[...].reshape(NX, NZL, NY, width)
+        low = part - rounded
+        low = jnp.concatenate([low[..., :side], low[..., side:]], axis=2)
+        low_part[q] = low.astype(BF16)
+
+    def low_rows(low):
+        low = low.astype(F32)
+        return jnp.concatenate([low[:NY], low[NY:]], axis=1)
 
     px_copies, pz_copies = [], []
     for q in range(2):
@@ -212,11 +201,9 @@
             for k in range(1, NX)
         ])
 
-        @pl.when(rest_x["src"])
+        @pl.when(lead_mate)
         def _():
-            part = part_buf[...].reshape(NX, NZL * NY, width)
-            lx_buf[q] = (part - px_buf[q].astype(F32)).astype(BF16)
-            send_rest(rest_x, q)
+            keep_low(q, px_buf[q].astype(F32).reshape(NX, NZL, NY, width))
 
         part_buf[...] = lax.dot_general(pair_q, met_ref[...], down, preferred_element_type=F32)
         for k in range(NZL):
@@ -227,12 +214,17 @@
             for k in range(1, NZL)
         ])
 
-        @pl.when(rest_z["src"])
+        @pl.when(lead)
         def _():
-            for k in range(NZL):
-                part = part_buf[...].reshape(NX, NZL, NY, width)[:, k].reshape(NX * NY, width)
-                lz_buf[q, k] = (part - pz_buf[q, k].astype(F32)).astype(BF16)
-            send_rest(rest_z, q)
+            part = part_buf[...]
+            keep_low(q, part.astype(BF16).astype(F32).reshape(NX, NZL, NY, width))
+
+        for role, leads in enumerate((lead, lead_mate)):
+
+            @pl.when(leads)
+            def _():
+                for copy in low_copies(role, q):
+                    copy.start()
 
     def summed(own, inbox, count):
         total = own.astype(F32)
@@ -245,7 +237,6 @@
             copy.wait_recv()
         total = summed(pz_buf[q, zl], lambda k: pz_in[q, k], NZL - 1)
         sx_buf[q] = total.reshape(NX, NY, width)
-        add_rest(rest_z, q, sx_buf)
         if q == 1:
             sx_copies = [
                 send(sx_buf.at[:, lax.rem(x + k, NX)], sx_in.at[k - 1], x_peers[k - 1])
@@ -255,30 +246,44 @@
             copy.wait_recv()
         total = summed(px_buf[q, x], lambda k: px_in[q, k], NX - 1)
         sz_buf[q] = total.reshape(NZL, NY, width)
-        add_rest(rest_x, q, sz_buf)
     sz_copies = []
     for k in range(NZL):
         to_zl = lax.rem(zl + k, NZL)
         sz_copies.append(send(sz_buf.at[:, to_zl], sz_in.at[k], device(zl=to_zl, c=mate)))
+    halves = ((0, zh), (1, 1 - zh))
     for copy in sx_copies:
         copy.wait_recv()
     total = summed(sx_buf[:, x], lambda k: sx_in[k], NX - 1)
-    out_ref[c, zh], out_ref[c, 1 - zh] = total[0], total[1]
+    for q, at in halves:
+        out_ref[c, at] = total[q]
+
+    @pl.when(lead)
+    def _():
+        for q, at in halves:
+            out_ref[c, at] += low_rows(low_part[q, x, zl])
+
+    @pl.when(jnp.logical_not(lead))
+    def _():
+        for q, at in halves:
+            low_copy(0, q, 1, 0).wait_recv()
+            out_ref[c, at] += low_rows(low_in[0, q])
+
     for copy in sz_copies:
         copy.wait_recv()
     total = summed(sz_in[0], lambda k: sz_in[k + 1], NZL - 1)
-    out_ref[mate, zh], out_ref[mate, 1 - zh] = total[0], total[1]
-
-    for rest in (rest_x, rest_z):
-
-        @pl.when(rest["src"])
+    for q, at in halves:
+        low_copy(1, q, 1, 0).wait_recv()
+        out_ref[mate, at] = total[q] + low_rows(low_in[1, q])
+
+    for copy in copies:
+        copy.wait_send()
+    for role, leads in enumerate((lead, lead_mate)):
+
+        @pl.when(leads)
         def _():
             for q in range(2):
-                for k in range(1, rest["size"]):
-                    rest_copy(rest, q, k).wait_send()
-
-    for copy in copies:
-        copy.wait_send()
+                for copy in low_copies(role, q):
+                    copy.wait_send()
 
 
 def shards(valence, conduction, points, inverse_metric):
@@ -312,10 +317,8 @@
             pltpu.VMEM((2, NX - 1, NZL * NY, width), BF16),
             pltpu.VMEM((2, NZL, NX * NY, width), BF16),
             pltpu.VMEM((2, NZL - 1, NX * NY, width), BF16),
-            pltpu.VMEM((2, NX, NZL * NY, width), BF16),
-            pltpu.VMEM((2, NZL * NY, width), BF16),
-            pltpu.VMEM((2, NZL, NX * NY, width), BF16),
-            pltpu.VMEM((2, NX * NY, width), BF16),
+            pltpu.VMEM((2, NX, NZL, 2 * NY, width // 2), BF16),
+            pltpu.VMEM((2, 2, 2 * NY, width // 2), BF16),
             pltpu.VMEM((2, NX, NY, width), F32),
             pltpu.VMEM((NX - 1, 2, NY, width), F32),
             pltpu.VMEM((2, NZL, NY, width), F32),
@@ -323,7 +326,7 @@
             pltpu.SemaphoreType.DMA((COPIES,)),
             pltpu.SemaphoreType.DMA((COPIES,)),
             pltpu.SemaphoreType.DMA((4,)),
-            pltpu.SemaphoreType.DMA((2, 2, NX - 1)),
+            pltpu.SemaphoreType.DMA((2, NX * NZL)),
             pltpu.SemaphoreType.DMA((2, 2)),
         ],
         compiler_params=pltpu.CompilerParams(

time: 81.1 us -> 80.4 us (level); the launches traced: 80.9 us -> 78.8 us
  Pallas kernels: 79.4 us -> 77.3 us
    pallas_call x1, Pallas kernels: 79.4 us -> 77.3 us  [shards(): pl.pallas_call(kernel, out_shape=jax.ShapeDtypeStruct((2, 2, NY, width),...]
where the time goes in v4:
time: 80.4 us; the launch traced here: 78.8 us
  Pallas kernels  77.3 us (96%)
  other arithmetic  0.85 us (1%)
    pallas_call x1, Pallas kernels, shards(): pl.pallas_call(kernel, out_shape=jax.ShapeDtypeStruct((2, 2, NY, width),...  77.3 us

profile of v4, /device:TPU:1, one launch (start us, length us, event | category | flops | bytes accessed | tf_op | source)
XLA Modules:
  0.0 78.8 jit_solution(2119871245751778963)
XLA Ops:
  0.0 77.3 %shard_map.46 = f32[2,2,8,512]{3,2,1,0:T(8,128)} custom-call(s32[1,512]{1,0:T(1,128)} %bitcast.3, bf16[256,512]{1,0:T(8,128)(2,1)} %val_hbm.1, bf16[256,512]{1,0:T(8,128)(2,1)} %con_hbm.1, bf16[512,512]{1,0:T(8,128)(2,1)} %met_hbm.1), custom_call_target="tpu_custom_call" | custom-call | tf_op jit(solution)/shard_map/pallas_call | solution.py:294
  77.3 0.8 %convert_bitcast_fusion = bf16[8,2,2,512]{3,0,1,2:T(8,128)(2,1)S(1)} fusion(f32[2,2,8,512]{3,2,1,0:T(8,128)} %shard_map.46), kind=kLoop, calls=%fused_computation | loop fusion | flops 16384 | bytes 98304 | tf_op jit(solution)/shard_map/convert_element_type | solution.py:336
  78.2 0.6 convert_element_type.11
  (1 shorter events, 0.0 us)

commit v5 on v4

--- a/solution.py
+++ b/solution.py
@@ -96,6 +96,11 @@
 
     sides = (slice(0, width), slice(width, 2 * width))
     picks = [picked(hot, ref) for ref in (val_ref, con_ref)]
+    for copy in row_copies:
+        copy.wait_recv()
+    for k in range(NY):
+        zl_buf[zl, k : k + 1, :] = row_buf[k]
+    zl_copies = [send(zl_buf.at[zl], zl_buf.at[zl], peer) for peer in zl_peers]
     for n, ref in enumerate((val_mate, con_mate)):
         core_rows[n].wait_recv()
         pick = picks[n] + picked(hot_mate, ref)
@@ -108,12 +113,6 @@
         ]
         for h in range(2)
     ]
-
-    for copy in row_copies:
-        copy.wait_recv()
-    for k in range(NY):
-        zl_buf[zl, k : k + 1, :] = row_buf[k]
-    zl_copies = [send(zl_buf.at[zl], zl_buf.at[zl], peer) for peer in zl_peers]
 
     for copy in zl_copies:
         copy.wait_recv()

time: 80.4 us -> 80.9 us (level); the launches traced: 78.8 us -> 80.7 us
  Pallas kernels: 77.3 us -> 79.1 us
    pallas_call x1, Pallas kernels: 77.3 us -> 79.1 us  [shards(): pl.pallas_call(kernel, out_shape=jax.ShapeDtypeStruct((2, 2, NY, width),...]
where the time goes in v5:
time: 80.9 us; the launch traced here: 80.7 us
  Pallas kernels  79.1 us (98%)
  other arithmetic  0.85 us (1%)
    pallas_call x1, Pallas kernels, shards(): pl.pallas_call(kernel, out_shape=jax.ShapeDtypeStruct((2, 2, NY, width),...  79.1 us

profile of v5, /device:TPU:1, one launch (start us, length us, event | category | flops | bytes accessed | tf_op | source)
XLA Modules:
  0.0 80.7 jit_solution(8570744100107832815)
XLA Ops:
  0.0 79.1 %shard_map.46 = f32[2,2,8,512]{3,2,1,0:T(8,128)} custom-call(s32[1,512]{1,0:T(1,128)} %bitcast.3, bf16[256,512]{1,0:T(8,128)(2,1)} %val_hbm.1, bf16[256,512]{1,0:T(8,128)(2,1)} %con_hbm.1, bf16[512,512]{1,0:T(8,128)(2,1)} %met_hbm.1), custom_call_target="tpu_custom_call" | custom-call | tf_op jit(solution)/shard_map/pallas_call | solution.py:293
  79.1 0.8 %convert_bitcast_fusion = bf16[8,2,2,512]{3,0,1,2:T(8,128)(2,1)S(1)} fusion(f32[2,2,8,512]{3,2,1,0:T(8,128)} %shard_map.46), kind=kLoop, calls=%fused_computation | loop fusion | flops 16384 | bytes 98304 | tf_op jit(solution)/shard_map/convert_element_type | solution.py:335
  80.0 0.6 convert_element_type.11
  (1 shorter events, 0.0 us)
